TPU v7x, 32 devices: a whole 2x2x4 slice. The times are simulated.
32 devices in a mesh: dp: 8 (over y, x, core), mp: 4 (over z).
Axes of the slice: x: 2, y: 2, z: 4, core: 2. Of those that a mesh axis runs over, the one named last changes fastest.
Arguments:
- block_input: bfloat16 [8192, 1024], P('dp'), may hold values from -6 to 6
- layer_one_input: bfloat16 [8192, 1024], P('dp', 'mp'), may hold values from -6 to 6
- segment_ids: int32 [8, 1024], P('dp'), may hold values from 0 to 7, never falling along the last dimension, each value on 1 to 512 neighbouring positions
- grad_output: bfloat16 [8192, 1024], P('dp'), may hold values from -6 to 6
- norm_one: float32 [1024], replicated, may hold values from 0.1 to 1.9
- w_query: bfloat16 [1024, 1024], P(None, 'mp'), may hold values from -0.1875 to 0.1875
- w_key: bfloat16 [1024, 1024], P(None, 'mp'), may hold values from -0.1875 to 0.1875
- w_value: bfloat16 [1024, 1024], P(None, 'mp'), may hold values from -0.1875 to 0.1875
- w_out: bfloat16 [1024, 1024], P('mp'), may hold values from -1.5 to 1.5
- norm_two: float32 [1024], replicated, may hold values from 0.1 to 1.9
- w_gate: bfloat16 [1024, 2816], P(None, 'mp'), may hold values from -0.1875 to 0.1875
- w_up: bfloat16 [1024, 2816], P(None, 'mp'), may hold values from -0.1875 to 0.1875
- w_down: bfloat16 [2816, 1024], P('mp'), may hold values from -0.109375 to 0.109375
- w_value_one: bfloat16 [1024, 1024], P('mp'), may hold values from -0.1875 to 0.1875
Outputs:
- output: bfloat16 [8192, 1024], P('dp')
- grad_input: float32 [8192, 1024], P('dp')
- grad_layer_one_input: float32 [8192, 1024], P('dp', 'mp')
- grad_norm_one: float32 [1024], replicated
- grad_query: float32 [1024, 1024], P(None, 'mp')
- grad_key: float32 [1024, 1024], P(None, 'mp')
- grad_value: float32 [1024, 1024], P(None, 'mp')
- grad_out_proj: float32 [1024, 1024], P('mp')
- grad_norm_two: float32 [1024], replicated
- grad_gate: float32 [1024, 2816], P(None, 'mp')
- grad_up: float32 [1024, 2816], P(None, 'mp')
- grad_down: float32 [2816, 1024], P('mp')
- grad_value_one: float32 [1024, 1024], P('mp')
Inputs may be any that keep to these rules, and one draw needn't show every extreme that they name: `segment_ids`: non-decreasing along each sequence, each document 1 to 512 tokens, one of exactly 512 in every sequence.
All inputs are finite; a program needn't handle non-finite values.
Results may differ from a plain program's by a relative error of at most 0.012.
Values may be sent and summed in bfloat16 or wider, within the bound.
A program may use at most 128 MiB of HBM per device.

v0:
```python
import math

import jax
import jax.numpy as jnp
from jax import lax
from jax.sharding import PartitionSpec as P

HD = 64


EPSILON = 1e-06


def positions_of(segments):
    position = lax.broadcasted_iota(jnp.int32, segments.shape, 1)
    changed = (segments[:, 1:] != segments[:, :-1]).astype(jnp.int32)
    starts = jnp.concatenate([jnp.ones_like(segments[:, :1]), changed], axis=1)
    return position - lax.cummax(position * starts, axis=1)


def rope_tables(positions, width):
    half_width = width // 2
    rates = jnp.exp(jnp.arange(half_width, dtype=jnp.float32) * (-math.log(10000.0) / half_width))
    angles = positions.astype(jnp.float32)[:, None] * rates[None, :]
    return (jnp.cos(angles)[:, None, :], jnp.sin(angles)[:, None, :])


def rotate(tensor, cosine, sine_part, turn):
    half_width = tensor.shape[-1] // 2
    left_half = tensor[..., :half_width]
    right_half = tensor[..., half_width:]
    return jnp.concatenate(
        [
            left_half * cosine - turn * right_half * sine_part,
            right_half * cosine + turn * left_half * sine_part,
        ],
        axis=-1,
    )


def over_rows(left_side, right_side):
    return lax.dot_general(
        left_side, right_side, (((0,), (0,)), ((), ())), preferred_element_type=jnp.float32
    )


def against(left_side, right_side):
    return lax.dot_general(
        left_side, right_side, (((1,), (1,)), ((), ())), preferred_element_type=jnp.float32
    )


def norm_back(activations, scale_vec, gain_vec, grad_normed):
    grad_gain = jnp.sum(grad_normed * activations * scale_vec, axis=0)
    scaled = grad_normed * gain_vec
    inner = jnp.mean(scaled * activations, axis=-1, keepdims=True)
    return (grad_gain, scale_vec * scaled - activations * scale_vec * scale_vec * scale_vec * inner)


def masked_scores(q_block, key_rows, seg_block, seg_all, first_row, score_scale):
    block_rows = q_block.shape[0]
    scores = (
        jnp.einsum("qhd,khd->hqk", q_block, key_rows, preferred_element_type=jnp.float32)
        * score_scale
    )
    row_index = first_row + lax.broadcasted_iota(jnp.int32, (block_rows, key_rows.shape[0]), 0)
    col_index = lax.broadcasted_iota(jnp.int32, (block_rows, key_rows.shape[0]), 1)
    allowed = (seg_block[:, None] == seg_all[None, :]) & (col_index <= row_index)
    return jnp.where(allowed[None], scores, -1e30)


def attend_forward(queries, key_rows, values, seg_all, score_scale):
    row_count, head_count, width = queries.shape
    block_rows = min(512, row_count)

    def one_block(block_index):
        first_row = block_index * block_rows
        q_block = lax.dynamic_slice_in_dim(queries, first_row, block_rows, 0)
        seg_block = lax.dynamic_slice_in_dim(seg_all, first_row, block_rows, 0)
        scores = masked_scores(q_block, key_rows, seg_block, seg_all, first_row, score_scale)
        largest = jnp.max(scores, axis=-1, keepdims=True)
        raised = jnp.exp(scores - largest)
        summed = jnp.sum(raised, axis=-1, keepdims=True)
        weights = (raised / summed).astype(jnp.bfloat16)
        result = jnp.einsum("hqk,khd->qhd", weights, values, preferred_element_type=jnp.float32)
        return (result, (largest + jnp.log(summed))[..., 0])

    results, log_totals = lax.map(one_block, jnp.arange(row_count // block_rows, dtype=jnp.int32))
    return (results.reshape(row_count, head_count, width), log_totals)


def attend_backward(queries, key_rows, values, seg_all, log_totals, grad_attended, score_scale):
    row_count = queries.shape[0]
    block_rows = min(512, row_count)

    def one_block(carried, block_index):
        grad_keys, grad_values = carried
        first_row = block_index * block_rows
        q_block = lax.dynamic_slice_in_dim(queries, first_row, block_rows, 0)
        seg_block = lax.dynamic_slice_in_dim(seg_all, first_row, block_rows, 0)
        grad_block = lax.dynamic_slice_in_dim(grad_attended, first_row, block_rows, 0)
        scores = masked_scores(q_block, key_rows, seg_block, seg_all, first_row, score_scale)
        probs = jnp.exp(scores - log_totals[block_index][..., None])
        grad_probs = jnp.einsum(
            "qhd,khd->hqk", grad_block, values, preferred_element_type=jnp.float32
        )
        inner = jnp.sum(probs * grad_probs, axis=-1, keepdims=True)
        grad_scores = (probs * (grad_probs - inner)).astype(jnp.bfloat16)
        grad_query = (
            jnp.einsum("hqk,khd->qhd", grad_scores, key_rows, preferred_element_type=jnp.float32)
            * score_scale
        )
        grad_keys = (
            grad_keys
            + jnp.einsum("hqk,qhd->khd", grad_scores, q_block, preferred_element_type=jnp.float32)
            * score_scale
        )
        grad_values = grad_values + jnp.einsum(
            "hqk,qhd->khd",
            probs.astype(jnp.bfloat16),
            grad_block,
            preferred_element_type=jnp.float32,
        )
        return ((grad_keys, grad_values), grad_query)

    zero_rows = jnp.zeros(key_rows.shape, jnp.float32)
    (grad_keys, grad_values), grad_queries = lax.scan(
        one_block, (zero_rows, zero_rows), jnp.arange(row_count // block_rows, dtype=jnp.int32)
    )
    return (grad_queries.reshape(key_rows.shape), grad_keys, grad_values)


def on_device(
    block_input,
    layer_one_input,
    segment_ids,
    grad_output,
    norm_one,
    w_query,
    w_key,
    w_value,
    w_out,
    norm_two,
    w_gate,
    w_up,
    w_down,
    w_value_one,
):
    token_count = block_input.shape[0]
    head_count = w_query.shape[1] // HD
    score_scale = HD ** (-0.5)
    seg_all = segment_ids[0]
    cosine, sine_part = rope_tables(positions_of(segment_ids)[0], HD)
    share_rows = token_count // lax.axis_size("mp")
    share_start = lax.axis_index("mp") * share_rows
    inputs = block_input.astype(jnp.float32)
    scale_one = lax.rsqrt(jnp.mean(inputs * inputs, axis=-1, keepdims=True) + EPSILON)
    normed = (inputs * scale_one * norm_one).astype(jnp.bfloat16)
    queries = jnp.dot(normed, w_query, preferred_element_type=jnp.float32).reshape(
        token_count, head_count, HD
    )
    key_rows = jnp.dot(normed, w_key, preferred_element_type=jnp.float32).reshape(
        token_count, head_count, HD
    )
    own_values = jnp.dot(normed, w_value, preferred_element_type=jnp.float32)
    first_values = lax.psum_scatter(
        jnp.dot(layer_one_input, w_value_one, preferred_element_type=jnp.float32),
        "mp",
        scatter_dimension=1,
        tiled=True,
    )
    mixed_values = (
        (0.5 * own_values + 0.5 * first_values)
        .astype(jnp.bfloat16)
        .reshape(token_count, head_count, HD)
    )
    turned_q = rotate(queries, cosine, sine_part, 1.0).astype(jnp.bfloat16)
    turned_k = rotate(key_rows, cosine, sine_part, 1.0).astype(jnp.bfloat16)
    attended, log_totals = attend_forward(turned_q, turned_k, mixed_values, seg_all, score_scale)
    attended = attended.reshape(token_count, head_count * HD).astype(jnp.bfloat16)
    branch_one = jnp.dot(attended, w_out, preferred_element_type=jnp.float32)
    inputs_here = lax.dynamic_slice_in_dim(inputs, share_start, share_rows, 0)
    scale_one_here = lax.dynamic_slice_in_dim(scale_one, share_start, share_rows, 0)
    grad_rows = lax.dynamic_slice_in_dim(grad_output, share_start, share_rows, 0).astype(
        jnp.float32
    )
    residual = inputs_here + lax.psum_scatter(branch_one, "mp", scatter_dimension=0, tiled=True)
    scale_two = lax.rsqrt(jnp.mean(residual * residual, axis=-1, keepdims=True) + EPSILON)
    normed_two = (residual * scale_two * norm_two).astype(jnp.bfloat16)
    normed_two = lax.all_gather(normed_two, "mp", axis=0, tiled=True)
    gate_pre = jnp.dot(normed_two, w_gate, preferred_element_type=jnp.float32)
    up_pre = jnp.dot(normed_two, w_up, preferred_element_type=jnp.float32)
    sigmoid_gate = jax.nn.sigmoid(gate_pre)
    silu_gate = gate_pre * sigmoid_gate
    hidden = (silu_gate * up_pre).astype(jnp.bfloat16)
    branch_two = jnp.dot(hidden, w_down, preferred_element_type=jnp.float32)
    output_share = (
        residual
        + lax.psum_scatter(
            branch_two.astype(jnp.bfloat16), "mp", scatter_dimension=0, tiled=True
        ).astype(jnp.float32)
    ).astype(jnp.bfloat16)
    output = lax.all_gather(output_share, "mp", axis=0, tiled=True)
    grad_down = over_rows(hidden, grad_output)
    grad_hidden = against(grad_output, w_down)
    grad_gate_pre = (
        grad_hidden * up_pre * sigmoid_gate * (1.0 + gate_pre * (1.0 - sigmoid_gate))
    ).astype(jnp.bfloat16)
    grad_up_pre = (grad_hidden * silu_gate).astype(jnp.bfloat16)
    grad_gate = over_rows(normed_two, grad_gate_pre)
    grad_up = over_rows(normed_two, grad_up_pre)
    back_two = against(grad_gate_pre, w_gate) + against(grad_up_pre, w_up)
    grad_normed_two = lax.psum_scatter(back_two, "mp", scatter_dimension=0, tiled=True)
    grad_norm_two, grad_through_two = norm_back(residual, scale_two, norm_two, grad_normed_two)
    grad_residual = grad_rows + grad_through_two
    residual_low = grad_residual.astype(jnp.bfloat16)
    residual_low = lax.all_gather(residual_low, "mp", axis=0, tiled=True)
    grad_out_proj = over_rows(attended, residual_low)
    grad_attended = (
        against(residual_low, w_out).astype(jnp.bfloat16).reshape(token_count, head_count, HD)
    )
    grad_turned_q, grad_turned_k, grad_mixed = attend_backward(
        turned_q, turned_k, mixed_values, seg_all, log_totals, grad_attended, score_scale
    )
    grad_value_part = (0.5 * grad_mixed).reshape(token_count, head_count * HD).astype(jnp.bfloat16)
    grad_first_full = lax.all_gather(grad_value_part, "mp", axis=1, tiled=True)
    grad_queries = (
        rotate(grad_turned_q, cosine, sine_part, -1.0)
        .reshape(token_count, head_count * HD)
        .astype(jnp.bfloat16)
    )
    grad_keys = (
        rotate(grad_turned_k, cosine, sine_part, -1.0)
        .reshape(token_count, head_count * HD)
        .astype(jnp.bfloat16)
    )
    grad_query = over_rows(normed, grad_queries)
    grad_key = over_rows(normed, grad_keys)
    grad_value = over_rows(normed, grad_value_part)
    back_one = (
        against(grad_queries, w_query)
        + against(grad_keys, w_key)
        + against(grad_value_part, w_value)
    )
    grad_normed = lax.psum_scatter(back_one, "mp", scatter_dimension=0, tiled=True)
    grad_norm_one, grad_through_one = norm_back(inputs_here, scale_one_here, norm_one, grad_normed)
    gain_rows = jnp.concatenate([grad_norm_one, grad_norm_two])[None, :]
    grad_input, gain_all = (
        lax.all_gather(grad_residual + grad_through_one, "mp", axis=0, tiled=True),
        lax.all_gather(gain_rows, "mp", axis=0, tiled=True),
    )
    gain_total = jnp.sum(gain_all, axis=0)
    width = norm_one.shape[0]
    grad_norm_one = gain_total[:width]
    grad_norm_two = gain_total[width:]
    grad_value_one = over_rows(layer_one_input, grad_first_full)
    grad_layer_one_input = against(grad_first_full, w_value_one)
    (
        grad_query,
        grad_key,
        grad_value,
        grad_out_proj,
        grad_value_one,
        grad_norm_one,
        grad_gate,
        grad_up,
        grad_down,
        grad_norm_two,
    ) = lax.psum(
        (
            grad_query,
            grad_key,
            grad_value,
            grad_out_proj,
            grad_value_one,
            grad_norm_one,
            grad_gate,
            grad_up,
            grad_down,
            grad_norm_two,
        ),
        "dp",
    )
    return (
        output,
        grad_input,
        grad_layer_one_input,
        grad_norm_one,
        grad_query,
        grad_key,
        grad_value,
        grad_out_proj,
        grad_norm_two,
        grad_gate,
        grad_up,
        grad_down,
        grad_value_one,
    )


def solution(mesh):
    return jax.shard_map(
        on_device,
        mesh=mesh,
        in_specs=(
            P("dp", None),
            P("dp", "mp"),
            P("dp", None),
            P("dp", None),
            P(),
            P(None, "mp"),
            P(None, "mp"),
            P(None, "mp"),
            P("mp", None),
            P(),
            P(None, "mp"),
            P(None, "mp"),
            P("mp", None),
            P("mp", None),
        ),
        out_specs=(
            P("dp", None),
            P("dp", None),
            P("dp", "mp"),
            P(),
            P(None, "mp"),
            P(None, "mp"),
            P(None, "mp"),
            P("mp", None),
            P(),
            P(None, "mp"),
            P(None, "mp"),
            P("mp", None),
            P("mp", None),
        ),
        check_vma=False,
    )
```

profile of v0, /device:TPU:0, one launch (start us, length us, event | category | flops | bytes accessed | tf_op | source)
XLA Modules:
  0.0 989.8 jit_solution(16211585150470690545)
XLA Ops:
  7.2 4.1 fusion.46
  20.1 70.9 %reduce-scatter.6.cloned.1.call-done = f32[1024,256]{0,1:T(8,128)} async-done(((f32[1024,1024]{0,1:T(8,128)}), f32[1024,256]{0,1:T(8,128)}) %reduce-scatter.6.cloned.1.call-update) | async-done | bytes 1048592 | tf_op jit(solution)/shard_map/reduce_scatter | solution.py:166
  91.0 2.9 fusion.39
  94.0 22.0 %while.27 = (s32[]{:T(128)}, bf16[2,512,4,64]{1,3,2,0:T(8,128)(2,1)}, f32[2,4,512]{2,1,0:T(4,128)}, s32[2]{0:T(128)S(1)}, s32[1024]{0:T(1024)S(1)}, /*index=5*/s...) while((s32[]{:T(128)}, ...), condition=%wide.region_7.8_spmd, body=%wide.region_4.0_spmd.sunk | while | flops 563608064 | bytes 35600724 | solution.py:88
  95.9 2.8 fusion.139
  101.1 3.0 fusion.141
  106.9 2.8 fusion.139
  112.1 3.0 fusion.141
  118.4 2.8 fusion.47
  122.8 2.4 convert_element_type.78
  125.2 73.4 %reduce-scatter.8.cloned.1.call-done = f32[256,1024]{1,0:T(8,128)} async-done(((f32[1024,1024]{1,0:T(8,128)}), f32[256,1024]{1,0:T(8,128)}) %reduce-scatter.8.cloned.1.call-update) | async-done | bytes 1048592 | tf_op jit(solution)/shard_map/reduce_scatter | solution.py:187
  201.6 46.4 %all-gather.7.cloned.1.call-done = bf16[1024,1024]{1,0:T(8,128)(2,1)} async-done(((bf16[256,1024]{1,0:T(8,128)(2,1)}), bf16[1024,1024]{1,0:T(8,128)(2,1)}) %all-gather.7.cloned.1.call-update) | async-done | bytes 2097168 | tf_op jit(solution)/shard_map/all_gather | solution.py:190
  247.9 3.8 fusion.48
  253.6 3.9 multiply_convert_fusion.2
  259.3 3.9 convolution_add_fusion
  263.3 4.5 convolution_convert_fusion
  267.9 71.0 %reduce-scatter.12.cloned.1.call-done = f32[256,1024]{1,0:T(8,128)} async-done(((f32[1024,1024]{1,0:T(8,128)}), f32[256,1024]{1,0:T(8,128)}) %reduce-scatter.12.cloned.1.call-update) | async-done | bytes 1048592 | tf_op jit(solution)/shard_map/reduce_scatter | solution.py:213
  340.4 45.7 %reduce-scatter.10.cloned.1.call-done = bf16[256,1024]{1,0:T(8,128)(2,1)} async-done(((bf16[1024,1024]{1,0:T(8,128)(2,1)}), bf16[256,1024]{1,0:T(8,128)(2,1)}) %reduce-scatter.10.cloned.1.call-update) | async-done | bytes 524304 | tf_op jit(solution)/shard_map/reduce_scatter | solution.py:199
  386.1 3.3 fusion.42
  389.8 45.1 %all-gather.11.cloned.1.call-done = bf16[1024,1024]{1,0:T(8,128)(2,1)} async-done(((bf16[256,1024]{1,0:T(8,128)(2,1)}), bf16[1024,1024]{1,0:T(8,128)(2,1)}) %all-gather.11.cloned.1.call-update) | async-done | bytes 2097168 | tf_op jit(solution)/shard_map/all_gather | solution.py:217
  434.9 3.2 convolution_convert_fusion.1
  438.1 77.0 %while.28 = (s32[]{:T(128)}, f32[1024,4,64]{0,2,1:T(8,128)S(1)}, f32[1024,4,64]{0,2,1:T(8,128)}, f32[2,512,4,64]{1,0,3,2:T(2,128)}, s32[2]{0:T(128)S(1)}, /*inde...) while((s32[]{:T(128)}, f32[1024,4,64]{0,2,1:T(8,128)S(1)}, ...), condition=%wide.region_15.16_spmd.clone, body=%wide.region_13.15_spmd.clone.sunk | while | flops 1376647680 | bytes 120658352 | solution.py:127
  440.0 4.6 fusion.151
  446.6 5.7 multiply_reduce_fusion.8
  452.6 2.4 multiply_convert_fusion.8
  457.0 10.4 %dynamic_update_slice.19 = f32[2,512,4,64]{1,0,3,2:T(2,128)} dynamic-update-slice(f32[2,512,4,64]{1,0,3,2:T(2,128)} %get-tuple-element.503, f32[1,512,4,64]{1,0,3,2:T(1,128)S(1)} %copy.53, s32[]{:T(128)} %get-tuple-element.500, s32[]{:T(128)} %constant.52.clone.1..sunk.1, s32[]{:T(128)} %constant.52.clone.1..sunk.1, s32[]{:T(128)} %constant.52.clone.1..sunk.1) | dynamic-update-slice | bytes 1048580 | tf_op jit(solution)/shard_map/while/body/jit(dynamic_update_index_in_dim)/dynamic_update_slice | solution.py:88
  467.4 3.2 fusion.153
  470.6 5.8 fusion.154
  478.4 4.6 fusion.151
  485.0 5.7 multiply_reduce_fusion.8
  495.4 10.4 %dynamic_update_slice.19 = f32[2,512,4,64]{1,0,3,2:T(2,128)} dynamic-update-slice(f32[2,512,4,64]{1,0,3,2:T(2,128)} %get-tuple-element.503, f32[1,512,4,64]{1,0,3,2:T(1,128)S(1)} %copy.53, s32[]{:T(128)} %get-tuple-element.500, s32[]{:T(128)} %constant.52.clone.1..sunk.1, s32[]{:T(128)} %constant.52.clone.1..sunk.1, s32[]{:T(128)} %constant.52.clone.1..sunk.1) | dynamic-update-slice | bytes 1048580 | tf_op jit(solution)/shard_map/while/body/jit(dynamic_update_index_in_dim)/dynamic_update_slice | solution.py:88
  505.7 3.2 fusion.153
  509.0 6.1 fusion.154
  522.8 2.8 add_add_fusion
  527.0 5.0 fusion.58
  532.0 3.2 fusion.59
  535.2 3.3 fusion.60
  545.4 16.7 %all-gather.15.cloned.1.call-done = bf16[1024,1024]{0,1:T(8,128)(2,1)} async-done(((bf16[1024,256]{0,1:T(8,128)(2,1)}), bf16[1024,1024]{0,1:T(8,128)(2,1)}) %all-gather.15.cloned.1.call-update) | async-done | bytes 2097168 | tf_op jit(solution)/shard_map/all_gather | solution.py:226
  562.1 3.4 convolution_bitcast_fusion
  566.4 74.1 %reduce-scatter.14.cloned.1.call-done = f32[256,1024]{1,0:T(8,128)} async-done(((f32[1024,1024]{1,0:T(8,128)}), f32[256,1024]{1,0:T(8,128)}) %reduce-scatter.14.cloned.1.call-update) | async-done | bytes 1048592 | tf_op jit(solution)/shard_map/reduce_scatter | solution.py:245
  642.3 3.0 subtract_add_fusion
  645.4 43.3 %all-gather.9.cloned.1.call-done = bf16[1024,1024]{1,0:T(8,128)(2,1)} async-done(((bf16[256,1024]{1,0:T(8,128)(2,1)}), bf16[1024,1024]{1,0:T(8,128)(2,1)}) %all-gather.9.cloned.1.call-update) | async-done | bytes 2097168 | tf_op jit(solution)/shard_map/all_gather | solution.py:203
  688.6 2.8 fusion.53
  691.4 13.2 %all-gather = f32[8192]{0:T(1024)S(1)} all-gather(f32[2048]{0:T(1024)S(1)} %pad_maximum_fusion.4), channel_id=2, replica_groups=mesh['dp'=8,'mp'=4] {'mp'}, dimensions={0}, use_global_device_ids=true | all-gather | bytes 40960 | tf_op jit(solution)/shard_map/all_gather | solution.py:250
  704.7 13.6 %all-reduce = (f32[1024]{0:T(1024)}, f32[1024]{0:T(1024)}) all-reduce(f32[1024]{0:T(1024)S(1)} %get-tuple-element.302, f32[1024]{0:T(1024)S(1)} %get-tuple-element.301), channel_id=1, replica_groups=mesh['dp'=8,'mp'=4] {'dp'}, use_global_device_ids=true, to_apply=%region_21.22 | all-reduce | flops 2048 | bytes 16384 | tf_op jit(solution)/shard_map/psum | solution.py:269
  718.3 165.2 %all-reduce.4.cloned.1.call-done = (f32[1024,256]{1,0:T(8,128)}, f32[1024,256]{1,0:T(8,128)}, f32[1024,256]{1,0:T(8,128)}, f32[256,1024]{1,0:T(8,128)}, f32[1024...) async-done(((f32[1024,256]{1,0:T(8,128)}, f32[1024,256]{1,0:T(8,128)}, f32[1024,256]{1,0:T(8,128)}, f32[256,1024]{1,0:T(8,128)}, ...) | async-done | bytes 13893648 | tf_op jit(solution)/shard_map/psum | solution.py:269
  883.5 2.5 copy.40
  886.0 80.5 %all-gather.13.cloned.1.call-done = f32[1024,1024]{1,0:T(8,128)} async-done(((f32[256,1024]{1,0:T(8,128)}), f32[1024,1024]{1,0:T(8,128)}) %all-gather.13.cloned.1.call-update) | async-done | bytes 4194320 | tf_op jit(solution)/shard_map/all_gather | solution.py:249
  (254 shorter events, 74.3 us)
Async XLA Ops:
  7.2 246.4 %copy-start = (bf16[704,1024]{1,0:T(8,128)(2,1)S(1)}, bf16[704,1024]{1,0:T(8,128)(2,1)}, u32[]{:S(2)}) copy-start(bf16[704,1024]{1,0:T(8,128)(2,1)} %param.30) | copy-start | bytes 4325380
  7.2 83.8 %reduce-scatter.6.cloned.1.call-start = ((), (), s32[]{:S(2)}) async-start(), calls=%async_computation.5 | async-start | bytes 5242880 | tf_op jit(solution)/shard_map/reduce_scatter | solution.py:166
  11.3 4.6 copy-start.47
  11.3 187.3 %reduce-scatter.8.cloned.1.call-start = ((), (), s32[]{:S(2)}) async-start(), calls=%async_computation.6 | async-start | bytes 5242880 | tf_op jit(solution)/shard_map/reduce_scatter | solution.py:187
  16.5 74.5 %copy-start.3 = (bf16[1024,1024]{1,0:T(8,128)(2,1)}, bf16[1024,1024]{1,0:T(8,128)(2,1)S(1)}, u32[]{:S(2)}) copy-start(bf16[1024,1024]{1,0:T(8,128)(2,1)S(1)} %multiply_convert_fusion.1) | copy-start | bytes 6291460
  94.0 24.4 %copy-start.38 = (bf16[256,1024]{1,0:T(8,128)(2,1)S(1)}, bf16[256,1024]{1,0:T(8,128)(2,1)}, u32[]{:S(2)}) copy-start(bf16[256,1024]{1,0:T(8,128)(2,1)} %param.26) | copy-start | bytes 1572868
  101.1 3.1 copy-start.44
  112.1 3.1 copy-start.44
  121.2 126.7 %all-gather.7.cloned.1.call-start = ((), (), s32[]{:S(2)}) async-start(), calls=%async_computation.7 | async-start | bytes 2621440 | tf_op jit(solution)/shard_map/all_gather | solution.py:190
  125.2 75.2 %copy-start.46 = (f32[1024]{0:T(1024)S(1)}, f32[1024]{0:T(1024)}, u32[]{:S(2)}) copy-start(f32[1024]{0:T(1024)} %param.27) | copy-start | bytes 12292
  201.3 137.6 %reduce-scatter.12.cloned.1.call-start = ((), (), s32[]{:S(2)}) async-start(), calls=%async_computation.10 | async-start | bytes 5242880 | tf_op jit(solution)/shard_map/reduce_scatter | solution.py:213
  247.9 3.8 copy-start.50
  247.9 3.8 copy-start.53
  253.6 3.9 copy-start.52
  263.3 122.9 %reduce-scatter.10.cloned.1.call-start = ((), (), s32[]{:S(2)}) async-start(), calls=%async_computation.8 | async-start | bytes 2621440 | tf_op jit(solution)/shard_map/reduce_scatter | solution.py:199
  267.9 167.0 %all-gather.11.cloned.1.call-start = ((), (), s32[]{:S(2)}) async-start(), calls=%async_computation.11 | async-start | bytes 2621440 | tf_op jit(solution)/shard_map/all_gather | solution.py:217
  389.4 172.7 %all-gather.15.cloned.1.call-start = ((), (), s32[]{:S(2)}) async-start(), calls=%async_computation.14 | async-start | bytes 2621440 | tf_op jit(solution)/shard_map/all_gather | solution.py:226
  389.7 48.3 %copy-start.5 = (bf16[1024,4,64]{0,2,1:T(8,128)(2,1)S(1)}, bf16[1024,4,64]{0,2,1:T(8,128)(2,1)}, u32[]{:S(2)}) copy-start(bf16[1024,4,64]{0,2,1:T(8,128)(2,1)} %get-tuple-element.586) | copy-start | bytes 1572868
  389.7 48.3 %copy-start.6 = (bf16[1024,4,64]{0,2,1:T(8,128)(2,1)S(1)}, bf16[1024,4,64]{0,2,1:T(8,128)(2,1)}, u32[]{:S(2)}) copy-start(bf16[1024,4,64]{0,2,1:T(8,128)(2,1)} %get-tuple-element.587) | copy-start | bytes 1572868
  389.7 48.3 %copy-start.11 = (bf16[1024,4,64]{0,2,1:T(8,128)(2,1)S(1)}, bf16[1024,4,64]{0,2,1:T(8,128)(2,1)}, u32[]{:S(2)}) copy-start(bf16[1024,4,64]{0,2,1:T(8,128)(2,1)} %get-tuple-element.592) | copy-start | bytes 1572868
  389.8 48.3 %copy-start.45 = (f32[2,4,512]{2,1,0:T(4,128)S(1)}, f32[2,4,512]{2,1,0:T(4,128)}, u32[]{:S(2)}) copy-start(f32[2,4,512]{2,1,0:T(4,128)} %get-tuple-element.492) | copy-start | bytes 49156
  446.6 5.8 slice-start
  446.6 6.0 slice-start.1
  467.4 3.2 copy-start.19
  470.6 5.8 copy-start.12
  485.0 5.8 slice-start
  485.0 6.0 slice-start.1
  505.7 3.2 copy-start.19
  509.0 6.2 copy-start.12
  515.1 4.6 copy-start.33
  515.1 4.6 copy-start.41
  517.3 123.2 %reduce-scatter.14.cloned.1.call-start = ((), (), s32[]{:S(2)}) async-start(), calls=%async_computation.12 | async-start | bytes 5242880 | tf_op jit(solution)/shard_map/reduce_scatter | solution.py:245
  525.7 163.0 %all-gather.9.cloned.1.call-start = ((), (), s32[]{:S(2)}) async-start(), calls=%async_computation.9 | async-start | bytes 2621440 | tf_op jit(solution)/shard_map/all_gather | solution.py:203
  526.4 357.1 %all-reduce.4.cloned.1.call-start = ((), (), s32[]{:S(2)}) async-start(), calls=%async_computation.15 | async-start | bytes 27787264 | tf_op jit(solution)/shard_map/psum | solution.py:269
  527.0 5.0 copy-start.51
  527.0 5.0 copy-start.57
  532.0 3.2 copy-start.55
  535.2 3.3 copy-start.4
  543.7 18.4 %copy-start.30 = (bf16[1024,256]{1,0:T(8,128)(2,1)S(1)}, bf16[1024,256]{1,0:T(8,128)(2,1)}, u32[]{:S(2)}) copy-start(bf16[1024,256]{1,0:T(8,128)(2,1)} %param.19) | copy-start | bytes 1572868
  565.5 75.0 %copy-start.48 = (f32[1024]{0:T(1024)S(1)}, f32[1024]{0:T(1024)}, u32[]{:S(2)}) copy-start(f32[1024]{0:T(1024)} %param.22) | copy-start | bytes 12292
  565.5 76.9 %copy-start.18 = (f32[256,1024]{1,0:T(8,128)S(1)}, f32[256,1024]{1,0:T(8,128)}, u32[]{:S(2)}) copy-start(f32[256,1024]{1,0:T(8,128)} %get-tuple-element.278) | copy-start | bytes 3145732
  565.5 401.1 %all-gather.13.cloned.1.call-start = ((), (), s32[]{:S(2)}) async-start(), calls=%async_computation.13 | async-start | bytes 5242880 | tf_op jit(solution)/shard_map/all_gather | solution.py:249
  642.3 46.3 %copy-start.16 = (bf16[1024,1024]{0,1:T(8,128)(2,1)S(1)}, bf16[1024,1024]{0,1:T(8,128)(2,1)}, u32[]{:S(2)}) copy-start(bf16[1024,1024]{0,1:T(8,128)(2,1)} %all-gather.15.cloned.1.call-done) | copy-start | bytes 6291460
  691.4 275.2 %copy-start.28 = (bf16[1024,1024]{1,0:T(8,128)(2,1)S(1)}, bf16[1024,1024]{1,0:T(8,128)(2,1)}, u32[]{:S(2)}) copy-start(bf16[1024,1024]{1,0:T(8,128)(2,1)} %all-gather.9.cloned.1.call-done) | copy-start | bytes 6291460
  966.6 2.9 copy-start.17
  969.5 3.1 copy-start.36
  971.6 2.9 copy-start.34
  978.4 4.4 copy-start.1
  (34 other events, 65.6 us)
Sparse Core Ops, SparseCore 0:
  11.5 79.4 reduce-scatter.5
  121.3 77.2 reduce-scatter.7
  201.5 46.4 all-gather.6
  263.4 75.4 reduce-scatter.11
  341.7 44.3 reduce-scatter.9
  389.5 45.2 all-gather.10
  517.4 44.6 all-gather.14
  565.0 75.4 reduce-scatter.13
  642.1 46.4 all-gather.8
  695.1 188.3 all-reduce.3
  885.7 80.8 all-gather.12
where the time goes:
time: 1000 us; the launch traced here: 990 us
  waiting for transfers between devices  733 us (73%)
  matrix products  117 us (12%)
  local copies, waits for them, and re-layouts  56.5 us (6%)
  other arithmetic  33.9 us (3%)
  blocking collectives  26.9 us (3%)
  between operations  14.8 us (1%)
    psum x1, waiting for transfers between devices, on_device(): lax.psum((grad_query, grad_key, grad_value, grad_out_proj, grad_value_one...  165 us
    all_gather x1, waiting for transfers between devices, on_device(): lax.all_gather(grad_residual + grad_through_one, 'mp', axis=0, tiled=True)  80.5 us
    reduce_scatter x1, waiting for transfers between devices, on_device(): lax.psum_scatter(back_one, 'mp', scatter_dimension=0, tiled=True)  74.1 us
    reduce_scatter x1, waiting for transfers between devices, on_device(): lax.psum_scatter(branch_one, 'mp', scatter_dimension=0, tiled=True)  73.4 us
    reduce_scatter x1, waiting for transfers between devices, on_device(): lax.psum_scatter(back_two, 'mp', scatter_dimension=0, tiled=True)  71 us
    reduce_scatter x1, waiting for transfers between devices, on_device(): lax.psum_scatter(jnp.dot(layer_one_input, w_value_one, preferred_element_...  70.9 us
    all_gather x1, waiting for transfers between devices, on_device(): normed_two = lax.all_gather(normed_two, 'mp', axis=0, tiled=True)  46.4 us
    reduce_scatter x1, waiting for transfers between devices, on_device(): lax.psum_scatter(branch_two.astype(jnp.bfloat16), 'mp', scatter_dimension...  45.7 us
  transfers between devices with their start and end apart: 11, of which 11 were waited for; matrix products, arithmetic and copies ran while one was open for 6% of the time, Pallas kernels for 0%

commit v1 on v0

--- a/solution.py
+++ b/solution.py
@@ -164,11 +164,13 @@
     )
     own_values = jnp.dot(normed, w_value, preferred_element_type=jnp.float32)
     first_values = lax.psum_scatter(
-        jnp.dot(layer_one_input, w_value_one, preferred_element_type=jnp.float32),
+        jnp.dot(layer_one_input, w_value_one, preferred_element_type=jnp.float32).astype(
+            jnp.bfloat16
+        ),
         "mp",
         scatter_dimension=1,
         tiled=True,
-    )
+    ).astype(jnp.float32)
     mixed_values = (
         (0.5 * own_values + 0.5 * first_values)
         .astype(jnp.bfloat16)
@@ -184,7 +186,9 @@
     grad_rows = lax.dynamic_slice_in_dim(grad_output, share_start, share_rows, 0).astype(
         jnp.float32
     )
-    residual = inputs_here + lax.psum_scatter(branch_one, "mp", scatter_dimension=0, tiled=True)
+    residual = inputs_here + lax.psum_scatter(
+        branch_one.astype(jnp.bfloat16), "mp", scatter_dimension=0, tiled=True
+    ).astype(jnp.float32)
     scale_two = lax.rsqrt(jnp.mean(residual * residual, axis=-1, keepdims=True) + EPSILON)
     normed_two = (residual * scale_two * norm_two).astype(jnp.bfloat16)
     normed_two = lax.all_gather(normed_two, "mp", axis=0, tiled=True)
@@ -210,7 +214,9 @@
     grad_gate = over_rows(normed_two, grad_gate_pre)
     grad_up = over_rows(normed_two, grad_up_pre)
     back_two = against(grad_gate_pre, w_gate) + against(grad_up_pre, w_up)
-    grad_normed_two = lax.psum_scatter(back_two, "mp", scatter_dimension=0, tiled=True)
+    grad_normed_two = lax.psum_scatter(
+        back_two.astype(jnp.bfloat16), "mp", scatter_dimension=0, tiled=True
+    ).astype(jnp.float32)
     grad_norm_two, grad_through_two = norm_back(residual, scale_two, norm_two, grad_normed_two)
     grad_residual = grad_rows + grad_through_two
     residual_low = grad_residual.astype(jnp.bfloat16)
@@ -242,11 +248,15 @@
         + against(grad_keys, w_key)
         + against(grad_value_part, w_value)
     )
-    grad_normed = lax.psum_scatter(back_one, "mp", scatter_dimension=0, tiled=True)
+    grad_normed = lax.psum_scatter(
+        back_one.astype(jnp.bfloat16), "mp", scatter_dimension=0, tiled=True
+    ).astype(jnp.float32)
     grad_norm_one, grad_through_one = norm_back(inputs_here, scale_one_here, norm_one, grad_normed)
     gain_rows = jnp.concatenate([grad_norm_one, grad_norm_two])[None, :]
     grad_input, gain_all = (
-        lax.all_gather(grad_residual + grad_through_one, "mp", axis=0, tiled=True),
+        lax.all_gather(
+            (grad_residual + grad_through_one).astype(jnp.bfloat16), "mp", axis=0, tiled=True
+        ).astype(jnp.float32),
         lax.all_gather(gain_rows, "mp", axis=0, tiled=True),
     )
     gain_total = jnp.sum(gain_all, axis=0)
@@ -255,32 +265,33 @@
     grad_norm_two = gain_total[width:]
     grad_value_one = over_rows(layer_one_input, grad_first_full)
     grad_layer_one_input = against(grad_first_full, w_value_one)
+    grad_norm_one, grad_norm_two = lax.psum((grad_norm_one, grad_norm_two), "dp")
+    summed = lax.psum(
+        tuple(
+            part.astype(jnp.bfloat16)
+            for part in (
+                grad_query,
+                grad_key,
+                grad_value,
+                grad_out_proj,
+                grad_value_one,
+                grad_gate,
+                grad_up,
+                grad_down,
+            )
+        ),
+        "dp",
+    )
     (
         grad_query,
         grad_key,
         grad_value,
         grad_out_proj,
         grad_value_one,
-        grad_norm_one,
         grad_gate,
         grad_up,
         grad_down,
-        grad_norm_two,
-    ) = lax.psum(
-        (
-            grad_query,
-            grad_key,
-            grad_value,
-            grad_out_proj,
-            grad_value_one,
-            grad_norm_one,
-            grad_gate,
-            grad_up,
-            grad_down,
-            grad_norm_two,
-        ),
-        "dp",
-    )
+    ) = tuple(part.astype(jnp.float32) for part in summed)
     return (
         output,
         grad_input,

time: 1000 us -> 744 us (0.74)
  waiting for transfers between devices: 733 us -> 471 us
  other arithmetic: 33.9 us -> 54.6 us
  local copies, waits for them, and re-layouts: 56.5 us -> 43.7 us
    reduce_scatter x3, waiting for transfers between devices: 219 us -> 123 us  [the longest x1 42.7 us: on_device(): lax.psum_scatter(back_two.astype(jnp.bfloat16), 'mp', scatter_dimension=0...]
    psum x1, waiting for transfers between devices: 165 us -> 83.8 us  [on_device(): lax.psum(tuple((part.astype(jnp.bfloat16) for part in (grad_query, grad_k...]
    all_gather x1, waiting for transfers between devices: 80.5 us -> 35.3 us  [on_device(): lax.all_gather((grad_residual + grad_through_one).astype(jnp.bfloat16), '...]
    reduce_scatter x1, waiting for transfers between devices: 70.9 us -> 37.6 us  [on_device(): lax.psum_scatter(jnp.dot(layer_one_input, w_value_one, preferred_element_...]
    convert_element_type x0 -> x9, other arithmetic: none -> 19 us  [the longest x7 11.5 us: on_device(): part.astype(jnp.float32)]
    unnamed x113 -> x105, local copies, waits for them, and re-layouts: 24.2 us -> 7 us
  transfers between devices with their start and end apart: 11 -> 11, of which waited for: 11 -> 11; matrix products, arithmetic and copies ran while one was open for 6% -> 10% of each run, Pallas kernels for 0% -> 0%
where the time goes in v1:
time: 744 us; the launch traced here: 733 us
  waiting for transfers between devices  471 us (63%)
  matrix products  114 us (15%)
  other arithmetic  54.6 us (7%)
  local copies, waits for them, and re-layouts  43.7 us (6%)
  blocking collectives  27.1 us (4%)
  between operations  14.6 us (2%)
    psum x1, waiting for transfers between devices, on_device(): lax.psum(tuple((part.astype(jnp.bfloat16) for part in (grad_query, grad_k...  83.8 us
    all_gather x1, waiting for transfers between devices, on_device(): normed_two = lax.all_gather(normed_two, 'mp', axis=0, tiled=True)  45.2 us
    all_gather x1, waiting for transfers between devices, on_device(): residual_low = lax.all_gather(residual_low, 'mp', axis=0, tiled=True)  44.9 us
    reduce_scatter x1, waiting for transfers between devices, on_device(): lax.psum_scatter(branch_two.astype(jnp.bfloat16), 'mp', scatter_dimension...  43.8 us
    reduce_scatter x1, waiting for transfers between devices, on_device(): lax.psum_scatter(back_two.astype(jnp.bfloat16), 'mp', scatter_dimension=0...  42.7 us
    all_gather x1, waiting for transfers between devices, on_device(): output = lax.all_gather(output_share, 'mp', axis=0, tiled=True)  42.2 us
    reduce_scatter x1, waiting for transfers between devices, on_device(): lax.psum_scatter(back_one.astype(jnp.bfloat16), 'mp', scatter_dimension=0...  41.5 us
    reduce_scatter x1, waiting for transfers between devices, on_device(): lax.psum_scatter(branch_one.astype(jnp.bfloat16), 'mp', scatter_dimension...  39.2 us
  transfers between devices with their start and end apart: 11, of which 11 were waited for; matrix products, arithmetic and copies ran while one was open for 10% of the time, Pallas kernels for 0%

profile of v1, /device:TPU:0, one launch (start us, length us, event | category | flops | bytes accessed | tf_op | source)
XLA Modules:
  0.0 732.8 jit_solution(10183581578058343862)
XLA Ops:
  7.2 3.4 convolution_convert_fusion.1
  19.9 37.6 %reduce-scatter.6.cloned.1.call-done = bf16[1024,256]{0,1:T(8,128)(2,1)} async-done(((bf16[1024,1024]{0,1:T(8,128)(2,1)}), bf16[1024,256]{0,1:T(8,128)(2,1)}) %reduce-scatter.6.cloned.1.call-update) | async-done | bytes 524304 | tf_op jit(solution)/shard_map/reduce_scatter | solution.py:166
  57.5 2.6 fusion.39
  60.1 19.2 %while.27 = (s32[]{:T(128)}, bf16[2,512,4,64]{1,3,2,0:T(8,128)(2,1)S(1)}, f32[2,4,512]{2,1,0:T(4,128)}, s32[2]{0:T(128)S(1)}, s32[1024]{0:T(1024)S(1)}, /*index=...) while((s32[]{:T(128)}, ...), condition=%wide.region_7.8_spmd, body=%wide.region_4.0_spmd.sunk | while | flops 563608064 | bytes 29309188 | solution.py:88
  66.7 3.0 fusion.148
  76.3 3.0 fusion.148
  83.0 4.1 convert_element_type.159
  87.0 39.2 %reduce-scatter.8.cloned.1.call-done = bf16[256,1024]{1,0:T(8,128)(2,1)} async-done(((bf16[1024,1024]{1,0:T(8,128)(2,1)}), bf16[256,1024]{1,0:T(8,128)(2,1)}) %reduce-scatter.8.cloned.1.call-update) | async-done | bytes 524304 | tf_op jit(solution)/shard_map/reduce_scatter | solution.py:189
  129.3 45.2 %all-gather.7.cloned.1.call-done = bf16[1024,1024]{1,0:T(8,128)(2,1)} async-done(((bf16[256,1024]{1,0:T(8,128)(2,1)}), bf16[1024,1024]{1,0:T(8,128)(2,1)}) %all-gather.7.cloned.1.call-update) | async-done | bytes 2097168 | tf_op jit(solution)/shard_map/all_gather | solution.py:194
  174.5 3.8 fusion.62
  180.1 3.9 multiply_convert_fusion.2
  185.8 3.3 add_convert_fusion.1
  189.2 42.7 %reduce-scatter.12.cloned.1.call-done = bf16[256,1024]{1,0:T(8,128)(2,1)} async-done(((bf16[1024,1024]{1,0:T(8,128)(2,1)}), bf16[256,1024]{1,0:T(8,128)(2,1)}) %reduce-scatter.12.cloned.1.call-update) | async-done | bytes 524304 | tf_op jit(solution)/shard_map/reduce_scatter | solution.py:217
  233.9 2.4 fusion.58
  236.8 44.9 %all-gather.11.cloned.1.call-done = bf16[1024,1024]{1,0:T(8,128)(2,1)} async-done(((bf16[256,1024]{1,0:T(8,128)(2,1)}), bf16[1024,1024]{1,0:T(8,128)(2,1)}) %all-gather.11.cloned.1.call-update) | async-done | bytes 2097168 | tf_op jit(solution)/shard_map/all_gather | solution.py:223
  281.7 3.1 convolution_convert_fusion.11
  285.4 86.1 %while.28 = (s32[]{:T(128)}, f32[1024,4,64]{0,2,1:T(8,128)S(1)}, f32[1024,4,64]{0,2,1:T(8,128)}, f32[2,512,4,64]{1,0,3,2:T(2,128)}, s32[2]{0:T(128)}, /*index=5*...) while((s32[]{:T(128)}, f32[1024,4,64]{0,2,1:T(8,128)S(1)}, ...), condition=%wide.region_15.16_spmd.clone, body=%wide.region_13.15_spmd.clone.sunk | while | flops 1376647680 | bytes 118561168 | solution.py:127
  288.0 5.5 fusion.158
  296.2 6.9 multiply_reduce_fusion.4
  303.0 2.4 multiply_convert_fusion.8
  308.8 10.4 %dynamic_update_slice.19 = f32[2,512,4,64]{1,0,3,2:T(2,128)} dynamic-update-slice(f32[2,512,4,64]{1,0,3,2:T(2,128)} %get-tuple-element.502, f32[1,512,4,64]{1,0,3,2:T(1,128)} %copy.53, s32[]{:T(128)} %get-tuple-element.499, s32[]{:T(128)} %constant.52.clone.1..sunk.1, s32[]{:T(128)} %constant.52.clone.1..sunk.1, s32[]{:T(128)} %constant.52.clone.1..sunk.1) | dynamic-update-slice | bytes 1048580 | tf_op jit(solution)/shard_map/while/body/jit(dynamic_update_index_in_dim)/dynamic_update_slice | solution.py:88
  319.2 3.3 fusion.160
  322.5 5.8 fusion.161
  330.9 5.5 fusion.158
  339.1 6.9 multiply_reduce_fusion.4
  345.9 2.4 multiply_convert_fusion.8
  351.7 10.4 %dynamic_update_slice.19 = f32[2,512,4,64]{1,0,3,2:T(2,128)} dynamic-update-slice(f32[2,512,4,64]{1,0,3,2:T(2,128)} %get-tuple-element.502, f32[1,512,4,64]{1,0,3,2:T(1,128)} %copy.53, s32[]{:T(128)} %get-tuple-element.499, s32[]{:T(128)} %constant.52.clone.1..sunk.1, s32[]{:T(128)} %constant.52.clone.1..sunk.1, s32[]{:T(128)} %constant.52.clone.1..sunk.1) | dynamic-update-slice | bytes 1048580 | tf_op jit(solution)/shard_map/while/body/jit(dynamic_update_index_in_dim)/dynamic_update_slice | solution.py:88
  362.1 3.3 fusion.160
  365.4 6.1 fusion.161
  373.7 3.1 reshape.338
  383.0 4.5 convolution_convert_fusion.2
  387.8 5.0 convolution_convert_fusion.5
  392.8 2.8 convolution_convert_fusion.3
  395.6 2.8 convolution_convert_fusion.4
  404.8 13.7 %all-gather.15.cloned.1.call-done = bf16[1024,1024]{0,1:T(8,128)(2,1)} async-done(((bf16[1024,256]{0,1:T(8,128)(2,1)}), bf16[1024,1024]{0,1:T(8,128)(2,1)}) %all-gather.15.cloned.1.call-update) | async-done | bytes 2097168 | tf_op jit(solution)/shard_map/all_gather | solution.py:232
  418.5 3.1 fusion.44
  422.6 41.5 %reduce-scatter.14.cloned.1.call-done = bf16[256,1024]{1,0:T(8,128)(2,1)} async-done(((bf16[1024,1024]{1,0:T(8,128)(2,1)}), bf16[256,1024]{1,0:T(8,128)(2,1)}) %reduce-scatter.14.cloned.1.call-update) | async-done | bytes 524304 | tf_op jit(solution)/shard_map/reduce_scatter | solution.py:251
  466.4 43.8 %reduce-scatter.10.cloned.1.call-done = bf16[256,1024]{1,0:T(8,128)(2,1)} async-done(((bf16[1024,1024]{1,0:T(8,128)(2,1)}), bf16[256,1024]{1,0:T(8,128)(2,1)}) %reduce-scatter.10.cloned.1.call-update) | async-done | bytes 524304 | tf_op jit(solution)/shard_map/reduce_scatter | solution.py:203
  510.2 3.4 fusion.47
  514.3 3.3 fusion.67
  517.7 13.1 %all-gather = f32[8192]{0:T(1024)S(1)} all-gather(f32[2048]{0:T(1024)S(1)} %pad_maximum_fusion.4), channel_id=2, replica_groups=mesh['dp'=8,'mp'=4] {'mp'}, dimensions={0}, use_global_device_ids=true | all-gather | bytes 40960 | tf_op jit(solution)/shard_map/all_gather | solution.py:260
  530.8 14.0 %all-reduce = (f32[1024]{0:T(1024)}, f32[1024]{0:T(1024)}) all-reduce(f32[1024]{0:T(1024)S(1)} %get-tuple-element.301, f32[1024]{0:T(1024)S(1)} %get-tuple-element.300), channel_id=1, replica_groups=mesh['dp'=8,'mp'=4] {'dp'}, use_global_device_ids=true, to_apply=%region_21.22 | all-reduce | flops 2048 | bytes 16384 | tf_op jit(solution)/shard_map/psum | solution.py:268
  544.9 83.8 %all-reduce.4.cloned.1.call-done = (bf16[256,1024]{0,1:T(8,128)(2,1)}, bf16[1024,256]{1,0:T(8,128)(2,1)}, bf16[1024,256]{1,0:T(8,128)(2,1)}, bf16[1024,256]{1,0:...) async-done(((bf16[256,1024]{0,1:T(8,128)(2,1)}, bf16[1024,256]{1,0:T(8,128)(2,1)}, ...) | async-done | bytes 6946832 | tf_op jit(solution)/shard_map/psum | solution.py:269
  628.7 3.4 convert_element_type.198
  641.4 35.3 %all-gather.13.cloned.1.call-done = bf16[1024,1024]{1,0:T(8,128)(2,1)} async-done(((bf16[256,1024]{1,0:T(8,128)(2,1)}), bf16[1024,1024]{1,0:T(8,128)(2,1)}) %all-gather.13.cloned.1.call-update) | async-done | bytes 2097168 | tf_op jit(solution)/shard_map/all_gather | solution.py:257
  676.7 4.1 convert_element_type.188
  680.8 42.2 %all-gather.9.cloned.1.call-done = bf16[1024,1024]{1,0:T(8,128)(2,1)} async-done(((bf16[256,1024]{1,0:T(8,128)(2,1)}), bf16[1024,1024]{1,0:T(8,128)(2,1)}) %all-gather.9.cloned.1.call-update) | async-done | bytes 2097168 | tf_op jit(solution)/shard_map/all_gather | solution.py:207
  723.0 3.1 copy.87
  (238 shorter events, 74.5 us)
Async XLA Ops:
  7.2 172.9 %copy-start = (bf16[704,1024]{1,0:T(8,128)(2,1)S(1)}, bf16[704,1024]{1,0:T(8,128)(2,1)}, u32[]{:S(2)}) copy-start(bf16[704,1024]{1,0:T(8,128)(2,1)} %param.30) | copy-start | bytes 4325380
  7.2 3.5 copy-start.20
  7.2 50.3 %reduce-scatter.6.cloned.1.call-start = ((), (), s32[]{:S(2)}) async-start(), calls=%async_computation.5 | async-start | bytes 2621440 | tf_op jit(solution)/shard_map/reduce_scatter | solution.py:166
  10.6 4.3 copy-start.38
  10.7 115.6 %reduce-scatter.8.cloned.1.call-start = ((), (), s32[]{:S(2)}) async-start(), calls=%async_computation.6 | async-start | bytes 2621440 | tf_op jit(solution)/shard_map/reduce_scatter | solution.py:189
  13.7 3.5 copy-start.42
  15.0 4.4 copy-start.21
  19.9 40.2 %copy-start.30 = (bf16[2,512,4,64]{1,3,2,0:T(8,128)(2,1)S(1)}, bf16[2,512,4,64]{1,3,2,0:T(8,128)(2,1)}, u32[]{:S(2)}) copy-start(bf16[2,512,4,64]{1,3,2,0:T(8,128)(2,1)} %custom-call.2) | copy-start | bytes 1572868
  79.3 3.5 copy-start.2
  79.4 3.5 copy-start.7
  82.9 91.5 %all-gather.7.cloned.1.call-start = ((), (), s32[]{:S(2)}) async-start(), calls=%async_computation.7 | async-start | bytes 2621440 | tf_op jit(solution)/shard_map/all_gather | solution.py:194
  87.0 40.8 %copy-start.37 = (f32[1024]{0:T(1024)S(1)}, f32[1024]{0:T(1024)}, u32[]{:S(2)}) copy-start(f32[1024]{0:T(1024)} %param.27) | copy-start | bytes 12292
  127.8 106.0 %copy-start.3 = (f32[256,1024]{1,0:T(8,128)}, f32[256,1024]{1,0:T(8,128)S(1)}, u32[]{:S(2)}) copy-start(f32[256,1024]{1,0:T(8,128)S(1)} %get-tuple-element.278) | copy-start | bytes 3145732
  127.9 106.0 %copy-start.40 = (f32[256]{0:T(256)}, f32[256]{0:T(256)S(1)}, u32[]{:S(2)}) copy-start(f32[256]{0:T(256)S(1)} %add_rsqrt_fusion.1) | copy-start | bytes 3076
  129.0 102.9 %reduce-scatter.12.cloned.1.call-start = ((), (), s32[]{:S(2)}) async-start(), calls=%async_computation.10 | async-start | bytes 2621440 | tf_op jit(solution)/shard_map/reduce_scatter | solution.py:217
  174.4 3.8 copy-start.46
  174.4 3.8 copy-start.50
  180.1 3.9 copy-start.49
  189.1 92.6 %copy-start.32 = (bf16[256,1024]{1,0:T(8,128)(2,1)S(1)}, bf16[256,1024]{1,0:T(8,128)(2,1)}, u32[]{:S(2)}) copy-start(bf16[256,1024]{1,0:T(8,128)(2,1)} %param.26) | copy-start | bytes 1572868
  189.1 92.5 %all-gather.11.cloned.1.call-start = ((), (), s32[]{:S(2)}) async-start(), calls=%async_computation.11 | async-start | bytes 2621440 | tf_op jit(solution)/shard_map/all_gather | solution.py:223
  233.8 51.0 %copy-start.44 = (f32[256]{0:T(256)}, f32[256]{0:T(256)S(1)}, u32[]{:S(2)}) copy-start(f32[256]{0:T(256)S(1)} %broadcast_multiply_fusion.2) | copy-start | bytes 3076
  236.3 182.2 %all-gather.15.cloned.1.call-start = ((), (), s32[]{:S(2)}) async-start(), calls=%async_computation.14 | async-start | bytes 2621440 | tf_op jit(solution)/shard_map/all_gather | solution.py:232
  296.2 6.9 slice-start
  296.2 6.9 slice-start.1
  319.2 3.3 copy-start.10
  339.1 6.9 slice-start
  339.1 6.9 slice-start.1
  362.1 3.3 copy-start.10
  371.5 5.3 copy-start.22
  371.5 5.3 copy-start.34
  373.7 90.4 %reduce-scatter.14.cloned.1.call-start = ((), (), s32[]{:S(2)}) async-start(), calls=%async_computation.12 | async-start | bytes 2621440 | tf_op jit(solution)/shard_map/reduce_scatter | solution.py:251
  383.0 127.2 %reduce-scatter.10.cloned.1.call-start = ((), (), s32[]{:S(2)}) async-start(), calls=%async_computation.8 | async-start | bytes 2621440 | tf_op jit(solution)/shard_map/reduce_scatter | solution.py:203
  387.6 241.1 %all-reduce.4.cloned.1.call-start = ((), (), s32[]{:S(2)}) async-start(), calls=%async_computation.15 | async-start | bytes 13893632 | tf_op jit(solution)/shard_map/psum | solution.py:269
  387.8 5.0 copy-start.47
  387.8 5.0 copy-start.54
  403.3 15.2 %copy-start.33 = (bf16[1024,256]{1,0:T(8,128)(2,1)S(1)}, bf16[1024,256]{1,0:T(8,128)(2,1)}, u32[]{:S(2)}) copy-start(bf16[1024,256]{1,0:T(8,128)(2,1)} %param.19) | copy-start | bytes 1572868
  421.6 42.5 %copy-start.39 = (f32[1024]{0:T(1024)S(1)}, f32[1024]{0:T(1024)}, u32[]{:S(2)}) copy-start(f32[1024]{0:T(1024)} %param.22) | copy-start | bytes 12292
  421.6 88.6 %copy-start.8 = (bf16[256,1024]{1,0:T(8,128)(2,1)S(1)}, bf16[256,1024]{1,0:T(8,128)(2,1)}, u32[]{:S(2)}) copy-start(bf16[256,1024]{1,0:T(8,128)(2,1)} %reduce-scatter.12.cloned.1.call-done) | copy-start | bytes 1572868
  421.6 88.6 %copy-start.41 = (f32[256]{0:T(256)S(1)}, f32[256]{0:T(256)}, u32[]{:S(2)}) copy-start(f32[256]{0:T(256)} %copy-done.40) | copy-start | bytes 3076
  421.6 88.5 %copy-start.4 = (f32[256,1024]{1,0:T(8,128)S(1)}, f32[256,1024]{1,0:T(8,128)}, u32[]{:S(2)}) copy-start(f32[256,1024]{1,0:T(8,128)} %copy-done.3) | copy-start | bytes 3145732
  421.6 255.1 %all-gather.13.cloned.1.call-start = ((), (), s32[]{:S(2)}) async-start(), calls=%async_computation.13 | async-start | bytes 2621440 | tf_op jit(solution)/shard_map/all_gather | solution.py:257
  422.6 43.2 %copy-start.45 = (f32[256]{0:T(256)}, f32[256]{0:T(256)S(1)}, u32[]{:S(2)}) copy-start(f32[256]{0:T(256)S(1)} %dynamic-slice.3) | copy-start | bytes 3076
  466.4 47.9 %copy-start.15 = (bf16[256,1024]{1,0:T(8,128)(2,1)S(1)}, bf16[256,1024]{1,0:T(8,128)(2,1)}, u32[]{:S(2)}) copy-start(bf16[256,1024]{1,0:T(8,128)(2,1)} %param.31) | copy-start | bytes 1572868
  513.6 209.4 %all-gather.9.cloned.1.call-start = ((), (), s32[]{:S(2)}) async-start(), calls=%async_computation.9 | async-start | bytes 2621440 | tf_op jit(solution)/shard_map/all_gather | solution.py:207
  514.3 3.3 copy-start.43
  628.7 3.4 copy-start.19
  636.0 3.2 copy-start.26
  637.0 3.2 copy-start.25
  (26 other events, 46.6 us)
Sparse Core Ops, SparseCore 0:
  10.9 46.5 reduce-scatter.5
  83.0 43.1 reduce-scatter.7
  129.1 45.2 all-gather.6
  189.3 42.5 reduce-scatter.11
  236.4 45.2 all-gather.10
  373.8 44.6 all-gather.14
  421.5 42.5 reduce-scatter.13
  467.0 43.1 reduce-scatter.9
  516.1 112.5 all-reduce.3
  630.7 46.0 all-gather.12
  678.3 44.6 all-gather.8
